TPU v7x, 512 devices: a whole 4x8x8 slice. The times are simulated.
512 devices in a mesh: space: 64 (over y_lo, z, x), tm: 8 (over y_hi, core).
Axes of the slice: x: 4, y: 8 (y_hi: 4, y_lo: 2; y = y_hi * 2 + y_lo), z: 8, core: 2. Of those that a mesh axis runs over, the one named last changes fastest.
Arguments:
- strain: bfloat16 [3, 2112, 65536], P(None, 'tm', 'space'), may hold values from -400 to 400
- block_starts: int32 [64], replicated, may hold values from 0 to 2023, as said below
- bin_numbers: int32 [16], replicated, may hold values from 1 to 31
Outputs:
- upper_factor: float32 [16, 128, 128], replicated
- mode_basis: bfloat16 [16, 128, 3, 65536], P(None, None, None, ('space', 'tm'))
Inputs may be any that keep to these rules, and one draw needn't show every extreme that they name: `block_starts`: block b starts at b * 32 plus a shift of 0 to 7; the first block's shift is 0 and the last block's is 7.
All inputs are finite; a program needn't handle non-finite values.
Results may differ from a plain program's by a relative error of at most 0.009.
Values may be sent and summed in bfloat16 or wider, within the bound.
A program may use at most 64 MiB of HBM per device.

v0:
```python
import math

import jax
import jax.numpy as jnp
from jax import lax
from jax.sharding import PartitionSpec as P

NFFT = 64


def window_table(bin_numbers):
    sample_steps = jnp.arange(NFFT, dtype=jnp.int32)
    hann_taper = (
        1.0 - jnp.cos(2.0 * math.pi * sample_steps.astype(jnp.float32) / NFFT)
    ) / math.sqrt(1.5 * NFFT)
    phase_turns = (bin_numbers[:, None] * sample_steps[None, :] % NFFT).astype(jnp.float32)
    angle_rows = 2.0 * math.pi * phase_turns / NFFT
    stacked = jnp.stack(
        [hann_taper * jnp.cos(angle_rows), -hann_taper * jnp.sin(angle_rows)], axis=1
    )
    return stacked.reshape(2 * bin_numbers.shape[0], NFFT).astype(jnp.bfloat16)


def shards(strain, block_starts, bin_numbers):
    window_rows = window_table(bin_numbers)
    freq_count = bin_numbers.shape[0]
    block_count = block_starts.shape[0]
    order = 2 * block_count
    positions = block_starts[:, None] + jnp.arange(NFFT, dtype=jnp.int32)[None, :]
    segments = jnp.take(
        lax.all_to_all(strain, "tm", split_axis=2, concat_axis=1, tiled=True), positions, axis=1
    )
    spectrum = jnp.einsum(
        "kt,cbtp->kbcp", window_rows, segments, preferred_element_type=jnp.float32
    )
    local_points = spectrum.shape[3]
    columns_all = spectrum.reshape(freq_count, order, 3 * local_points)
    local_gram = jnp.einsum(
        "fjr,fkr->fjk", columns_all, columns_all, precision=lax.Precision.HIGHEST
    )
    row_total = 3.0 * local_points * lax.axis_size("space") * lax.axis_size("tm")
    summed = lax.psum(local_gram, ("space", "tm"))
    lower_factor = jnp.linalg.cholesky(summed / row_total)
    solved = lax.linalg.triangular_solve(lower_factor, columns_all, left_side=True, lower=True)
    mode_basis = solved.astype(jnp.bfloat16).reshape(freq_count, order, 3, local_points)
    return (jnp.swapaxes(lower_factor, 1, 2), mode_basis)


def solution(mesh):
    placed = (P(None, "tm", "space"), P(), P())
    return jax.shard_map(
        shards,
        mesh=mesh,
        in_specs=placed,
        out_specs=(P(), P(None, None, None, ("space", "tm"))),
        check_vma=False,
    )
```

profile of v0, /device:TPU:1, one launch (start us, length us, event | category | flops | bytes accessed | tf_op | source)
XLA Modules:
  0.0 803.6 jit_solution(1729191447162533374)
XLA Ops:
  7.2 5.3 copy.65
  12.5 10.6 %all-to-all-start = ((bf16[3,264,1024]{1,0,2:T(4,128)(2,1)}), bf16[3,264,1024]{1,0,2:T(4,128)(2,1)S(1)}, u32[]{:S(2)}, u32[]{:S(2)}) async-start(bf16[3,264,1024]{1,0,2:T(4,128)(2,1)} %copy.65), calls=%async_computation | async-start | bytes 6291456 | tf_op jit(solution)/shard_map/all_to_all | solution.py:31
  23.1 0.0 all-reduce.2.cloned.1.call-start
  23.1 0.0 copy-done.2
  23.1 0.1 multiply_convert_fusion.1
  23.3 0.0 copy-done.1
  23.3 0.1 compare_select_fusion
  23.4 0.1 reshape.226
  23.5 0.1 fusion.12
  23.6 70.8 %all-to-all-done = bf16[3,264,1024]{1,0,2:T(4,128)(2,1)S(1)} async-done(((bf16[3,264,1024]{1,0,2:T(4,128)(2,1)}), bf16[3,264,1024]{1,0,2:T(4,128)(2,1)S(1)}, u32[]{:S(2)}, u32[]{:S(2)}) %all-to-all-start) | async-done | bytes 1622048 | tf_op jit(solution)/shard_map/all_to_all | solution.py:31
  94.4 3.9 copy.82
  98.3 9.5 %copy.68 = bf16[3,2112,128]{2,0,1:T(4,128)(2,1)S(1)} copy(bf16[3,2112,128]{2,1,0:T(8,128)(2,1)} %bitcast.38) | data formatting | bytes 3244032 | tf_op jit(solution)/shard_map/all_to_all | solution.py:31
  107.7 28.6 %gather_fusion = bf16[4096,3,128]{2,1,0:T(4,128)(2,1)} fusion(bf16[3,2112,128]{2,0,1:T(4,128)(2,1)S(1)} %copy.68, s32[4096]{0:T(1024)S(1)} %broadcast_clamp_fusion), kind=kCustom, calls=%fused_computation | custom fusion | bytes 6307840 | tf_op jit(solution)/shard_map/jit(_take)/gather | solution.py:30
  136.4 4.2 fusion.3
  140.6 4.1 copy.71
  144.6 4.5 reshape.222
  149.2 5.1 fusion.21
  154.3 0.0 all-reduce.2.cloned.1.call-update
  154.4 272.8 %all-reduce.2.cloned.1.call-done = f32[16,128,128]{1,2,0:T(8,128)} async-done(((f32[16,128,128]{1,2,0:T(8,128)}), f32[16,128,128]{1,2,0:T(8,128)}) %all-reduce.2.cloned.1.call-update) | async-done | bytes 1048592 | tf_op jit(solution)/shard_map/psum | solution.py:42
  427.2 2.3 broadcast_multiply_fusion
  429.5 2.5 copy.73
  432.0 2.7 fusion.8
  434.7 189.0 %custom-call.7 = f32[16,128,128]{2,1,0:T(8,128)} custom-call(f32[16,128,128]{2,1,0:T(8,128)} %fusion.8), custom_call_target="Cholesky" | custom-call | tf_op jit(solution)/shard_map/jit(cholesky)/cholesky | solution.py:43
  623.7 1.3 select_reduce_fusion
  625.0 0.1 compare_reduce_fusion
  625.1 2.8 select_bitcast_fusion
  627.9 158.6 %custom-call.8 = f32[16,1,128,128]{2,3,1,0:T(8,128)} custom-call(f32[16,1,128,128]{3,2,1,0:T(8,128)} %get-tuple-element.16), custom_call_target="InvertDiagBlocksLowerTriangular" | custom-call | tf_op jit(solution)/shard_map/triangular_solve | solution.py:44
  786.5 5.4 convolution_convert_fusion
  791.9 2.0 copy.75
  793.9 1.6 copy.77
  795.5 0.0 copy-done
  795.5 1.3 copy.76
  (9 shorter events, 0.1 us)
Async XLA Ops:
  12.5 10.6 %copy-start.2 = (s32[16]{0:T(128)S(1)}, s32[16]{0:T(128)}, u32[]{:S(2)}) copy-start(s32[16]{0:T(128)} %param.5) | copy-start | bytes 196
  12.5 10.8 %copy-start.1 = (s32[64]{0:T(128)S(1)}, s32[64]{0:T(128)}, u32[]{:S(2)}) copy-start(s32[64]{0:T(128)} %param.4) | copy-start | bytes 772
  12.5 81.9 %all-to-all-start = ((bf16[3,264,1024]{1,0,2:T(4,128)(2,1)}), bf16[3,264,1024]{1,0,2:T(4,128)(2,1)S(1)}, u32[]{:S(2)}, u32[]{:S(2)}) async-start(bf16[3,264,1024]{1,0,2:T(4,128)(2,1)} %copy.65), calls=%async_computation | async-start | bytes 6291456 | tf_op jit(solution)/shard_map/all_to_all | solution.py:31
  23.1 404.1 %all-reduce.2.cloned.1.call-start = ((), (), s32[]{:S(2)}) async-start(), calls=%async_computation.1 | async-start | bytes 2097152 | tf_op jit(solution)/shard_map/psum | solution.py:42
  791.9 3.6 copy-start
Sparse Core Ops, SparseCore 0:
  154.4 272.6 all-reduce.1
where the time goes:
time: 805 us; the launch traced here: 804 us
  other arithmetic  357 us (44%)
  waiting for transfers between devices  344 us (43%)
  local copies, waits for them, and re-layouts  63.4 us (8%)
  matrix products  14.7 us (2%)
  between operations  14.1 us (2%)
  starting transfers between devices  10.6 us (1%)
    psum x1, waiting for transfers between devices, shards(): summed = lax.psum(local_gram, ('space', 'tm'))  273 us
    another operation x4, other arithmetic, shards(): lower_factor = jnp.linalg.cholesky(summed / row_total)  190 us
    another operation x2, other arithmetic, shards(): lax.linalg.triangular_solve(lower_factor, columns_all, left_side=True, lo...  161 us
    all_to_all x1, waiting for transfers between devices, shards(): lax.all_to_all(strain, 'tm', split_axis=2, concat_axis=1, tiled=True)  70.8 us
    gather x1, local copies, waits for them, and re-layouts, shards(): jnp.take(lax.all_to_all(strain, 'tm', split_axis=2, concat_axis=1, tiled=...  28.6 us
  transfers between devices with their start and end apart: 2, of which 2 were waited for; matrix products, arithmetic and copies ran while one was open for 0% of the time, Pallas kernels for 0%

commit v1 on v0

v1 whole, which is shorter than its diff:
```python
import functools
import math

import jax
import jax.numpy as jnp
from jax import lax
from jax.experimental import pallas as pl
from jax.experimental.pallas import tpu as pltpu
from jax.sharding import PartitionSpec as P

NFFT = 64
HOP = 32
MESH = pl.DeviceIdType.MESH
F32 = jnp.float32
BF16 = jnp.bfloat16

NX, NZ, NY, NT = 4, 8, 8, 8


def window_table(bin_numbers):
    sample_steps = jnp.arange(NFFT, dtype=jnp.int32)
    hann_taper = (
        1.0 - jnp.cos(2.0 * math.pi * sample_steps.astype(F32) / NFFT)
    ) / math.sqrt(1.5 * NFFT)
    phase_turns = (bin_numbers[:, None] * sample_steps[None, :] % NFFT).astype(F32)
    angle_rows = 2.0 * math.pi * phase_turns / NFFT
    stacked = jnp.stack(
        [hann_taper * jnp.cos(angle_rows), -hann_taper * jnp.sin(angle_rows)], axis=1
    )
    return stacked.reshape(2 * bin_numbers.shape[0], NFFT).astype(BF16)


def iota(shape, dim):
    return lax.broadcasted_iota(jnp.int32, shape, dim)


def dot(a, b):
    return jnp.dot(a, b, preferred_element_type=F32)


def dot_t(a, b):
    return lax.dot_general(a, b, (((1,), (1,)), ((), ())), preferred_element_type=F32)


def place():
    s, t = lax.axis_index("space"), lax.axis_index("tm")
    x = lax.rem(s, NX)
    z = lax.rem(lax.div(s, NX), NZ)
    ylo = lax.div(s, NX * NZ)
    core = lax.rem(t, 2)
    yhi = lax.div(t, 2)
    return s, t, x, z, ylo, core, yhi


def space_of(x, z, ylo):
    return (ylo * NZ + z) * NX + x


def remote(src, dst, send, recv, device):
    return pltpu.make_async_remote_copy(
        src_ref=src, dst_ref=dst, send_sem=send, recv_sem=recv,
        device_id=device, device_id_type=MESH,
    )


FAR_T = (4, 5, 3, 2, 6, 7, 1)
FAR_8 = (4, 3, 5, 2, 6, 1, 7)
FAR_4 = (2, 1, 3)


def build_windows(starts, window, amat, mmat):
    tile = (lax.rem(iota((NFFT, 512), 1), NFFT) == iota((NFFT, 512), 0)).astype(BF16)
    tiled = dot(window[...], tile).astype(BF16)
    spread = (lax.div(iota((256, 32), 0), 8) == iota((256, 32), 1)).astype(BF16)
    full = dot(spread, tiled)
    same = lax.rem(iota((256, 512), 0), 8) == lax.div(iota((256, 512), 1), NFFT)
    amat[...] = jnp.where(same, full, 0.0).astype(BF16)
    slot = iota((NFFT, 384), 1)
    when = jnp.where(slot < 264, slot, jnp.where(slot < 304, slot - 8, slot - 376))
    real = (slot < 264) | ((slot >= 272) & (slot < 304)) | ((slot >= 304) & (slot < 376))
    when = jnp.where(real, when, -100000) - iota((NFFT, 384), 0)
    for g in range(8):
        parts = []
        for b in range(8):
            begin = starts[8 * g + b] - 264 * g
            parts.append(jnp.where(when == begin, 1.0, 0.0).astype(BF16))
        pick = jnp.concatenate(parts, axis=0)
        mmat[g] = dot(amat[...], pick).astype(BF16)


def first_kernel(
    strain, starts, window, zout, gout,
    came, slab, amat, mmat, spec, zbuf, gram, packed, rc, sum4, rx, pz, rz, piece, ry, fin, gz,
    a_send, a_recv, own_sem, c_send, c_recv, x_send, x_recv, z_send, z_recv,
    y_send, y_recv, w_send, w_recv, out_sem,
):
    s, t, x, z, ylo, core, yhi = place()
    yy = yhi * 2 + ylo
    tm_peers = [(s, lax.rem(t + o, NT)) for o in range(1, NT)]
    x_peers = {o: (space_of(lax.rem(x + o, NX), z, ylo), t) for o in FAR_4}
    z_peers = {o: (space_of(x, lax.rem(z + o, NZ), ylo), t) for o in FAR_8}

    def y_peer(o):
        other = lax.rem(yy + o, NY)
        return (space_of(x, z, lax.rem(other, 2)), lax.div(other, 2) * 2 + core)

    y_peers = {o: y_peer(o) for o in FAR_8}
    mate = (s, t + 1 - 2 * core)

    barrier = pltpu.get_barrier_semaphore()
    odd = {o: y_peers[o] for o in (1, 3, 5, 7)}
    greeted = tm_peers + list(x_peers.values()) + list(z_peers.values()) + list(odd.values())
    for peer in greeted:
        pl.semaphore_signal(barrier, inc=1, device_id=peer, device_id_type=MESH)
    pl.semaphore_wait(barrier, len(greeted))

    sends = []
    for c in range(3):
        for o in FAR_T:
            to = lax.rem(t + o, NT)
            copy = remote(
                strain.at[c, :, pl.ds(pl.multiple_of(to * 128, 128), 128)],
                came.at[t, c], a_send.at[o, c], a_recv.at[o, c], (s, to),
            )
            copy.start()
            sends.append(copy)
    own = pltpu.make_async_copy(
        strain.at[:, :, pl.ds(pl.multiple_of(t * 128, 128), 128)], came.at[t], own_sem
    )
    own.start()

    build_windows(starts, window, amat, mmat)
    slab[...] = jnp.zeros_like(slab)
    own.wait()

    for c in range(3):
        for o in FAR_T:
            source = lax.rem(t + NT - o, NT)
            remote(
                came.at[source, c], came.at[source, c], a_send.at[o, c], a_recv.at[o, c], (s, source)
            ).wait_recv()
        for g in range(8):
            slab[g, 0:264, :] = came[g, c, :, :]
            if g < 7:
                slab[g, 272:304, :] = came[g + 1, c, 0:32, :]
            if g > 0:
                slab[g, 304:376, :] = came[g - 1, c, 192:264, :]
        for g in range(8):
            found = dot(mmat[g], slab[g])
            spec[:, 8 * g : 8 * g + 8, :] = found.reshape(32, 8, 128)

        def one(f, carry, c=c):
            rows = spec[pl.ds(2 * f, 2)].reshape(128, 128)
            high = rows.astype(BF16)
            low = (rows - high.astype(F32)).astype(BF16)
            both = jnp.concatenate([high, low], axis=0)
            zbuf[f, :, 128 * c : 128 * c + 128] = both
            quad = dot_t(both, both)
            new = (quad[:128, :128] + quad[128:, 128:]) + (quad[:128, 128:] + quad[128:, :128])
            if c == 0:
                gram[f] = new
            else:
                gram[f] = gram[f] + new
            return carry

        lax.fori_loop(0, 16, one, 0)
    save = pltpu.make_async_copy(zbuf, zout, out_sem)
    save.start()

    row, col = iota((128, 128), 0), iota((128, 128), 1)
    for q in range(8):
        first, second = gram[2 * q], gram[2 * q + 1]
        packed[q, 0:128, :] = jnp.where(row > col, first, second)
        diag = jnp.sum(jnp.where(row == col, first, 0.0), axis=0, keepdims=True)
        packed[q, 128:136, :] = jnp.broadcast_to(diag, (8, 128))

    for o in FAR_4 + (0,):
        xo = lax.rem(x + o, NX)
        copy = remote(packed.at[(1 - core) * 4 + xo], rc.at[xo], c_send.at[o], c_recv.at[o], mate)
        copy.start()
        sends.append(copy)
    for o in FAR_4:
        xo = lax.rem(x + o, NX)
        remote(packed.at[xo], rc.at[xo], c_send.at[o], c_recv.at[o], mate).wait_recv()
        sum4[xo] = packed[core * 4 + xo] + rc[xo]
        copy = remote(sum4.at[xo], rx.at[x], x_send.at[o], x_recv.at[o], x_peers[o])
        copy.start()
        sends.append(copy)
    remote(packed.at[x], rc.at[x], c_send.at[0], c_recv.at[0], mate).wait_recv()
    rx[x] = packed[core * 4 + x] + rc[x]
    for o in FAR_4:
        source = lax.rem(x + NX - o, NX)
        remote(sum4.at[source], rx.at[source], x_send.at[o], x_recv.at[o], x_peers[o]).wait_recv()
    mine = (rx[0] + rx[1]) + (rx[2] + rx[3])

    for i in range(NZ):
        pz[i, 0:16, :] = mine[16 * i : 16 * i + 16]
        pz[i, 16:24, :] = mine[128:136]
    for o in FAR_8:
        zo = lax.rem(z + o, NZ)
        copy = remote(pz.at[zo], rz.at[z], z_send.at[o], z_recv.at[o], z_peers[o])
        copy.start()
        sends.append(copy)
    rz[z] = pz[z]
    for o in FAR_8:
        source = lax.rem(z + NZ - o, NZ)
        remote(pz.at[source], rz.at[source], z_send.at[o], z_recv.at[o], z_peers[o]).wait_recv()
    piece[...] = ((rz[0] + rz[1]) + (rz[2] + rz[3])) + ((rz[4] + rz[5]) + (rz[6] + rz[7]))

    for o in FAR_8:
        copy = remote(piece, ry.at[yy], y_send.at[o], y_recv.at[o], y_peers[o])
        copy.start()
        sends.append(copy)
    ry[yy] = piece[...]
    for o in FAR_8:
        source = lax.rem(yy + NY - o, NY)
        remote(piece, ry.at[source], y_send.at[o], y_recv.at[o], y_peers[o]).wait_recv()
    fin[...] = ((ry[0] + ry[1]) + (ry[2] + ry[3])) + ((ry[4] + ry[5]) + (ry[6] + ry[7]))

    for o in FAR_8:
        copy = remote(fin, gz.at[z], w_send.at[o], w_recv.at[o], z_peers[o])
        copy.start()
        sends.append(copy)
    gz[z] = fin[...]
    for o in FAR_8:
        source = lax.rem(z + NZ - o, NZ)
        remote(fin, gz.at[source], w_send.at[o], w_recv.at[o], z_peers[o]).wait_recv()
    gout[...] = gz[...]

    for copy in sends:
        copy.wait_send()
    save.wait()


def factor_kernel(total_rows, g, out):
    lanes, subs = iota((8, 128), 1), iota((8, 128), 0)
    row, col = iota((128, 128), 0), iota((128, 128), 1)
    square = jnp.concatenate([g[i, 0:16, :] for i in range(NZ)], axis=0) * (1.0 / total_rows)
    spare = g[0, 16:17, :] * (1.0 / total_rows)
    turned = square.T
    first = jnp.where(row == col, spare, jnp.where(row > col, square, turned))
    second = jnp.where(row > col, turned, square)
    mats = [[m[8 * v : 8 * v + 8] for v in range(16)] for m in (first, second)]
    for j in range(128):
        v0, r = j // 8, j % 8
        here = lanes == j
        for m in mats:
            top = m[v0]
            column = jnp.broadcast_to(top[:, j : j + 1], (8, 128))
            pivot = jnp.broadcast_to(column[r : r + 1, :], (8, 128))
            root = lax.rsqrt(pivot)
            root = root * (1.5 - 0.5 * pivot * root * root)
            across = jnp.broadcast_to(top[r : r + 1, :], (8, 128))
            across = jnp.where(here, 1.0, across) * root
            scaled = across * root
            new = jnp.where(here, 0.0, top) - column * scaled
            m[v0] = jnp.where(subs > r, new, jnp.where(subs == r, across, top))
            for v in range(v0 + 1, 16):
                column = jnp.broadcast_to(m[v][:, j : j + 1], (8, 128))
                m[v] = jnp.where(here, 0.0, m[v]) - column * scaled
    for k in range(2):
        for v in range(16):
            out[k, 8 * v : 8 * v + 8, :] = mats[k][v]


def gather_kernel(mine, out, held, x_send, x_recv, c_send, c_recv):
    s, t, x, z, ylo, core, yhi = place()
    mate = (s, t + 1 - 2 * core)
    x_peers = {o: (space_of(lax.rem(x + o, NX), z, ylo), t) for o in FAR_4}
    barrier = pltpu.get_barrier_semaphore()
    for peer in list(x_peers.values()) + [mate]:
        pl.semaphore_signal(barrier, inc=1, device_id=peer, device_id_type=MESH)
    pl.semaphore_wait(barrier, 4)
    sends = []
    for o in FAR_4:
        copy = remote(mine, held.at[core * 4 + x], x_send.at[o], x_recv.at[o], x_peers[o])
        copy.start()
        sends.append(copy)
    copy = remote(mine, held.at[core * 4 + x], c_send.at[0], c_recv.at[0], mate)
    copy.start()
    sends.append(copy)
    held[core * 4 + x] = mine[...]
    for o in (1, 3, 2):
        slot = core * 4 + lax.rem(x + NX - o, NX)
        remote(mine, held.at[slot], x_send.at[o], x_recv.at[o], x_peers[o]).wait_recv()
        copy = remote(held.at[slot], held.at[slot], c_send.at[o], c_recv.at[o], mate)
        copy.start()
        sends.append(copy)
    for o in (0, 1, 3, 2):
        slot = (1 - core) * 4 + lax.rem(x + NX - o, NX)
        remote(mine, held.at[slot], c_send.at[o], c_recv.at[o], mate).wait_recv()
    out[...] = held[...]
    for copy in sends:
        copy.wait_send()


def apply_kernel(pk, zz, upper, basis):
    row, col = iota((128, 128), 0), iota((128, 128), 1)
    for k in range(2):
        both = pk[0, k]
        upper[k] = jnp.where(col > row, both, jnp.where(col == row, 1.0 / both, 0.0))
        inverse = jnp.where(col <= row, both, 0.0)
        high = inverse.astype(BF16)
        low = (inverse - high.astype(F32)).astype(BF16)
        twice = jnp.concatenate([high, high], axis=1)
        found = dot(twice, zz[k]) + dot(low, zz[k, 0:128, :])
        for c in range(3):
            basis[k, c] = found[:, 128 * c : 128 * c + 128].astype(BF16)


def shards(strain, block_starts, bin_numbers):
    window = window_table(bin_numbers)
    vmem = pl.BlockSpec(memory_space=pltpu.VMEM)
    hbm = pl.BlockSpec(memory_space=pl.ANY)
    dma = pltpu.SemaphoreType.DMA
    total_rows = 3.0 * 128 * lax.axis_size("space") * lax.axis_size("tm")
    zz, summed = pl.pallas_call(
        first_kernel,
        out_shape=(
            jax.ShapeDtypeStruct((16, 256, 384), BF16),
            jax.ShapeDtypeStruct((NZ, 24, 128), F32),
        ),
        in_specs=[hbm, pl.BlockSpec(memory_space=pltpu.SMEM), vmem],
        out_specs=(hbm, vmem),
        scratch_shapes=[
            pltpu.VMEM((NT, 3, 264, 128), BF16),
            pltpu.VMEM((8, 384, 128), BF16),
            pltpu.VMEM((256, 512), BF16),
            pltpu.VMEM((8, 256, 384), BF16),
            pltpu.VMEM((32, 64, 128), F32),
            pltpu.VMEM((16, 256, 384), BF16),
            pltpu.VMEM((16, 128, 128), F32),
            pltpu.VMEM((8, 136, 128), F32),
            pltpu.VMEM((4, 136, 128), F32),
            pltpu.VMEM((4, 136, 128), F32),
            pltpu.VMEM((4, 136, 128), F32),
            pltpu.VMEM((NZ, 24, 128), F32),
            pltpu.VMEM((NZ, 24, 128), F32),
            pltpu.VMEM((24, 128), F32),
            pltpu.VMEM((NY, 24, 128), F32),
            pltpu.VMEM((24, 128), F32),
            pltpu.VMEM((NZ, 24, 128), F32),
            dma((NT, 3)), dma((NT, 3)), dma,
            dma((4,)), dma((4,)), dma((4,)), dma((4,)),
            dma((8,)), dma((8,)), dma((8,)), dma((8,)), dma((8,)), dma((8,)), dma,
        ],
        compiler_params=pltpu.CompilerParams(
            collective_id=0, has_side_effects=True, vmem_limit_bytes=40 * 1024 * 1024
        ),
    )(strain, block_starts, window)
    factor = pl.pallas_call(
        functools.partial(factor_kernel, total_rows),
        out_shape=jax.ShapeDtypeStruct((2, 128, 128), F32),
        in_specs=[vmem],
        out_specs=vmem,
    )(summed)
    held = pl.pallas_call(
        gather_kernel,
        out_shape=jax.ShapeDtypeStruct((8, 2, 128, 128), F32),
        in_specs=[vmem],
        out_specs=vmem,
        scratch_shapes=[
            pltpu.VMEM((8, 2, 128, 128), F32),
            dma((4,)), dma((4,)), dma((4,)), dma((4,)),
        ],
        compiler_params=pltpu.CompilerParams(
            collective_id=1, has_side_effects=True, vmem_limit_bytes=16 * 1024 * 1024
        ),
    )(factor)
    upper, basis = pl.pallas_call(
        apply_kernel,
        grid=(8,),
        out_shape=(
            jax.ShapeDtypeStruct((16, 128, 128), F32),
            jax.ShapeDtypeStruct((16, 3, 128, 128), BF16),
        ),
        in_specs=[
            pl.BlockSpec((1, 2, 128, 128), lambda i: (i, 0, 0, 0)),
            pl.BlockSpec((2, 256, 384), lambda i: (i, 0, 0)),
        ],
        out_specs=(
            pl.BlockSpec((2, 128, 128), lambda i: (i, 0, 0)),
            pl.BlockSpec((2, 3, 128, 128), lambda i: (i, 0, 0, 0)),
        ),
    )(held, zz)
    return upper, jnp.transpose(basis, (0, 2, 1, 3))


def solution(mesh):
    placed = (P(None, "tm", "space"), P(), P())
    return jax.shard_map(
        shards,
        mesh=mesh,
        in_specs=placed,
        out_specs=(P(), P(None, None, None, ("space", "tm"))),
        check_vma=False,
    )
```

time: 805 us -> 125 us (0.16)
  other arithmetic: 357 us -> 0.84 us
  waiting for transfers between devices: 344 us -> 0 us
  Pallas kernels: 0 us -> 117 us
  local copies, waits for them, and re-layouts: 63.4 us -> 6.24 us
  matrix products: 14.7 us -> 0 us
  between operations: 14.1 us -> 0.69 us
  starting transfers between devices: 10.6 us -> 0 us
    another operation x7 -> x1, other arithmetic: 352 us -> 0.79 us  [the longest x4 190 us: shards(): lower_factor = jnp.linalg.cholesky(summed / row_total)]
    psum x1 -> x0, waiting for transfers between devices: 273 us -> none  [shards(): summed = lax.psum(local_gram, ('space', 'tm'))]
    pallas_call x0 -> x4, Pallas kernels: none -> 117 us  [the longest x1 76.2 us: shards(): pl.pallas_call(first_kernel, out_shape=(jax.ShapeDtypeStruct((16, 256, 38...]
    all_to_all x1 -> x0, waiting for transfers between devices: 70.8 us -> none  [shards(): lax.all_to_all(strain, 'tm', split_axis=2, concat_axis=1, tiled=True)]
    gather x1 -> x0, local copies, waits for them, and re-layouts: 28.6 us -> none  [shards(): jnp.take(lax.all_to_all(strain, 'tm', split_axis=2, concat_axis=1, tiled=...]
    all_to_all x2 -> x0, local copies, waits for them, and re-layouts: 13.3 us -> none  [shards(): lax.all_to_all(strain, 'tm', split_axis=2, concat_axis=1, tiled=True)]
    all_to_all x1 -> x0, starting transfers between devices: 10.6 us -> none  [shards(): lax.all_to_all(strain, 'tm', split_axis=2, concat_axis=1, tiled=True)]
    dot_general x2 -> x0, matrix products: 9.28 us -> none  [the longest x1 5.1 us: shards(): jnp.einsum('fjr,fkr->fjk', columns_all, columns_all, precision=lax.Precis...]
  transfers between devices with their start and end apart: 2 -> 0, of which waited for: 2 -> 0; matrix products, arithmetic and copies ran while one was open for 0% -> 0% of each run, Pallas kernels for 0% -> 0%
where the time goes in v1:
time: 125 us; the launch traced here: 124 us
  Pallas kernels  117 us (94%)
  local copies, waits for them, and re-layouts  6.24 us (5%)
    pallas_call x1, Pallas kernels, shards(): pl.pallas_call(first_kernel, out_shape=(jax.ShapeDtypeStruct((16, 256, 38...  76.2 us
    pallas_call x1, Pallas kernels, shards(): pl.pallas_call(functools.partial(factor_kernel, total_rows), out_shape=ja...  20.1 us
    pallas_call x1, Pallas kernels, shards(): pl.pallas_call(gather_kernel, out_shape=jax.ShapeDtypeStruct((8, 2, 128,...  13.3 us
    pallas_call x1, Pallas kernels, shards(): pl.pallas_call(apply_kernel, grid=(8,), out_shape=(jax.ShapeDtypeStruct((...  6.96 us
    unnamed x12, local copies, waits for them, and re-layouts  6.23 us

profile of v1, /device:TPU:1, one launch (start us, length us, event | category | flops | bytes accessed | tf_op | source)
XLA Modules:
  0.0 124.4 jit_solution(8832854657076639502)
XLA Ops:
  0.7 0.8 multiply_convert_fusion.1
  1.5 0.0 copy-start.2
  1.5 1.4 %copy-done.2 = bf16[3,264,1024]{2,1,0:T(8,128)(2,1)S(1)} copy-done((bf16[3,264,1024]{2,1,0:T(8,128)(2,1)S(1)}, bf16[3,264,1024]{2,1,0:T(8,128)(2,1)}, u32[]{:S(2)}) %copy-start.2) | copy-done | bytes 1622040
  2.9 0.0 copy-start.5
  2.9 0.7 copy-done.5
  3.6 76.2 %shard_map.50 = (bf16[16,256,384]{2,1,0:T(8,128)(2,1)S(1)}, f32[8,24,128]{2,1,0:T(8,128)S(1)}) custom-call(bf16[3,264,1024]{2,1,0:T(8,128)(2,1)S(1)} %copy-done.2, s32[64]{0:T(128)S(1)} %copy-done.5, bf16[32,64]{1,0:T(8,128)(2,1)S(1)} %bitcast.2), custom_call_target="tpu_custom_call" | custom-call | tf_op jit(solution)/shard_map/pallas_call | solution.py:317
  79.8 0.0 copy-start.1
  79.8 1.6 %copy-done.1 = bf16[16,256,384]{2,1,0:T(8,128)(2,1)} copy-done((bf16[16,256,384]{2,1,0:T(8,128)(2,1)}, bf16[16,256,384]{2,1,0:T(8,128)(2,1)S(1)}, u32[]{:S(2)}) %copy-start.1) | copy-done | bytes 3145752
  81.5 0.0 copy-start.4
  81.5 0.6 copy-done.4
  82.1 20.1 %shard_map.51.mine = f32[2,128,128]{2,1,0:T(8,128)} custom-call(f32[8,24,128]{2,1,0:T(8,128)} %copy-done.4), custom_call_target="tpu_custom_call" | custom-call | tf_op jit(solution)/shard_map/pallas_call | solution.py:351
  102.2 0.0 copy-start.3
  102.2 0.9 copy-done.3
  103.1 13.3 %shard_map.52.pk = f32[8,2,128,128]{3,2,1,0:T(8,128)S(1)} custom-call(f32[2,128,128]{2,1,0:T(8,128)S(1)} %copy-done.3), custom_call_target="tpu_custom_call" | custom-call | tf_op jit(solution)/shard_map/pallas_call | solution.py:357
  116.4 0.0 copy-start
  116.4 1.0 copy-done
  117.4 7.0 %shard_map.53 = (f32[16,128,128]{2,1,0:T(8,128)}, bf16[16,3,128,128]{3,2,1,0:T(8,128)(2,1)}) custom-call(f32[8,2,128,128]{3,2,1,0:T(8,128)} %copy-done, bf16[16,256,384]{2,1,0:T(8,128)(2,1)} %copy-done.1), custom_call_target="tpu_custom_call" | custom-call | tf_op jit(solution)/shard_map/pallas_call | solution.py:370
  (3 shorter events, 0.1 us)
Async XLA Ops:
  1.5 1.4 %copy-start.2 = (bf16[3,264,1024]{2,1,0:T(8,128)(2,1)S(1)}, bf16[3,264,1024]{2,1,0:T(8,128)(2,1)}, u32[]{:S(2)}) copy-start(bf16[3,264,1024]{2,1,0:T(8,128)(2,1)} %strain.1) | copy-start | bytes 4866052
  2.9 0.7 copy-start.5
  79.8 1.6 %copy-start.1 = (bf16[16,256,384]{2,1,0:T(8,128)(2,1)}, bf16[16,256,384]{2,1,0:T(8,128)(2,1)S(1)}, u32[]{:S(2)}) copy-start(bf16[16,256,384]{2,1,0:T(8,128)(2,1)S(1)} %get-tuple-element.7.zz) | copy-start | bytes 9437188
  81.5 0.6 copy-start.4
  102.2 0.9 copy-start.3
  116.4 1.0 copy-start

commit v2 on v1

v2 whole, which is shorter than its diff:
```python
import functools
import math

import jax
import jax.numpy as jnp
from jax import lax
from jax.experimental import pallas as pl
from jax.experimental.pallas import tpu as pltpu
from jax.sharding import PartitionSpec as P

NFFT = 64
HOP = 32
MESH = pl.DeviceIdType.MESH
F32 = jnp.float32
BF16 = jnp.bfloat16

NX, NZ, NY, NT = 4, 8, 8, 8


def iota(shape, dim):
    return lax.broadcasted_iota(jnp.int32, shape, dim)


def dot(a, b):
    return jnp.dot(a, b, preferred_element_type=F32)


def dot_t(a, b):
    return lax.dot_general(a, b, (((1,), (1,)), ((), ())), preferred_element_type=F32)


def place():
    s, t = lax.axis_index("space"), lax.axis_index("tm")
    x = lax.rem(s, NX)
    z = lax.rem(lax.div(s, NX), NZ)
    ylo = lax.div(s, NX * NZ)
    core = lax.rem(t, 2)
    yhi = lax.div(t, 2)
    return s, t, x, z, ylo, core, yhi


def space_of(x, z, ylo):
    return (ylo * NZ + z) * NX + x


def remote(src, dst, send, recv, device):
    return pltpu.make_async_remote_copy(
        src_ref=src, dst_ref=dst, send_sem=send, recv_sem=recv,
        device_id=device, device_id_type=MESH,
    )


FAR_T = ((2, 0), (2, 1), (1, 0), (1, 1), (3, 0), (3, 1), (0, 1))
FAR_8 = (4, 3, 5, 2, 6, 1, 7)
FAR_4 = (2, 1, 3)


def build_windows(starts, bins, amat, mmat):
    step = iota((32, NFFT), 1)
    freq = lax.div(iota((32, NFFT), 0), 2)
    turns = jnp.zeros((32, NFFT), jnp.int32)
    for f in range(16):
        turns = jnp.where(freq == f, bins[f], turns)
    angle = (2.0 * math.pi) * lax.rem(turns * step, NFFT).astype(F32) / NFFT
    taper = (1.0 - jnp.cos((2.0 * math.pi) * step.astype(F32) / NFFT)) / math.sqrt(1.5 * NFFT)
    real = lax.rem(iota((32, NFFT), 0), 2) == 0
    window = (taper * jnp.where(real, jnp.cos(angle), -jnp.sin(angle))).astype(BF16)
    tile = (lax.rem(iota((NFFT, 512), 1), NFFT) == iota((NFFT, 512), 0)).astype(BF16)
    tiled = dot(window, tile).astype(BF16)
    spread = (lax.div(iota((256, 32), 0), 8) == iota((256, 32), 1)).astype(BF16)
    full = dot(spread, tiled)
    same = lax.rem(iota((256, 512), 0), 8) == lax.div(iota((256, 512), 1), NFFT)
    amat[...] = jnp.where(same, full, 0.0).astype(BF16)
    slot = iota((NFFT, 384), 1)
    when = jnp.where(slot < 264, slot, jnp.where(slot < 304, slot - 8, slot - 376))
    known = (slot < 264) | ((slot >= 272) & (slot < 304)) | ((slot >= 304) & (slot < 376))
    when = jnp.where(known, when, -100000) - iota((NFFT, 384), 0)
    for g in range(8):
        parts = []
        for b in range(8):
            begin = starts[8 * g + b] - 264 * g
            parts.append(jnp.where(when == begin, 1.0, 0.0).astype(BF16))
        pick = jnp.concatenate(parts, axis=0)
        mmat[g] = dot(amat[...], pick).astype(BF16)


def first_kernel(
    total_rows,     strain, starts, bins, zout, out,
    came, slab, amat, mmat, spec, zbuf, gram, packed, rc, sum4, rx, pz, rz, piece, ry, fin, gz, held,
    a_send, a_recv, own_sem, c_send, c_recv, x_send, x_recv, z_send, z_recv,
    y_send, y_recv, w_send, w_recv, f_send, f_recv, m_send, m_recv, out_sem,
):
    s, t, x, z, ylo, core, yhi = place()
    yy = yhi * 2 + ylo
    def tm_peer(dy, dc):
        return lax.rem(yhi + dy, 4) * 2 + lax.rem(core + dc, 2)

    tm_peers = [(s, tm_peer(*o)) for o in FAR_T]
    x_peers = {o: (space_of(lax.rem(x + o, NX), z, ylo), t) for o in FAR_4}
    z_peers = {o: (space_of(lax.rem(x + 8 - o, NX), lax.rem(z + o, NZ), ylo), t) for o in FAR_8}
    line = {o: (space_of(x, lax.rem(z + o, NZ), ylo), t) for o in (1, 2, 6, 7)}
    own = lax.rem(x + z, NX)

    def y_peer(o):
        other = lax.rem(yy + o, NY)
        return (space_of(x, z, lax.rem(other, 2)), lax.div(other, 2) * 2 + core)

    y_peers = {o: y_peer(o) for o in FAR_8}
    mate = (s, t + 1 - 2 * core)

    barrier = pltpu.get_barrier_semaphore()
    odd = {o: y_peers[o] for o in (1, 3, 5, 7)}
    greeted = tm_peers + list(x_peers.values()) + list(z_peers.values()) + list(odd.values()) + list(line.values())
    for peer in greeted:
        pl.semaphore_signal(barrier, inc=1, device_id=peer, device_id_type=MESH)
    pl.semaphore_wait(barrier, len(greeted))

    sends = []
    for c in range(3):
        for o in FAR_T:
            to = tm_peer(*o)
            n = o[0] * 2 + o[1]
            copy = remote(
                strain.at[c, :, pl.ds(pl.multiple_of(to * 128, 128), 128)],
                came.at[t, c], a_send.at[n, c], a_recv.at[n, c], (s, to),
            )
            copy.start()
            sends.append(copy)
    stay = pltpu.make_async_copy(
        strain.at[:, :, pl.ds(pl.multiple_of(t * 128, 128), 128)], came.at[t], own_sem
    )
    stay.start()

    build_windows(starts, bins, amat, mmat)
    slab[...] = jnp.zeros_like(slab)
    stay.wait()

    for c in range(3):
        for o in FAR_T:
            source = tm_peer(4 - o[0], o[1])
            n = o[0] * 2 + o[1]
            remote(
                came.at[source, c], came.at[source, c], a_send.at[n, c], a_recv.at[n, c], (s, source)
            ).wait_recv()
        for g in range(8):
            slab[g, 0:264, :] = came[g, c, :, :]
            if g < 7:
                slab[g, 272:304, :] = came[g + 1, c, 0:32, :]
            if g > 0:
                slab[g, 304:376, :] = came[g - 1, c, 192:264, :]
        for g in range(8):
            found = dot(mmat[g], slab[g])
            spec[:, 8 * g : 8 * g + 8, :] = found.reshape(32, 8, 128)

        def one(f, carry, c=c):
            rows = spec[pl.ds(2 * f, 2)].reshape(128, 128)
            high = rows.astype(BF16)
            low = (rows - high.astype(F32)).astype(BF16)
            both = jnp.concatenate([high, low], axis=0)
            zbuf[f, :, 128 * c : 128 * c + 128] = both
            quad = dot_t(both, both)
            new = (quad[:128, :128] + quad[128:, 128:]) + (quad[:128, 128:] + quad[128:, :128])
            if c == 0:
                gram[f] = new
            else:
                gram[f] = gram[f] + new
            return carry

        lax.fori_loop(0, 16, one, 0)
    save = pltpu.make_async_copy(zbuf, zout, out_sem)
    save.start()

    row, col = iota((128, 128), 0), iota((128, 128), 1)
    for q in range(8):
        first, second = gram[2 * q], gram[2 * q + 1]
        packed[q, 0:128, :] = jnp.where(row > col, first, second)
        diag = jnp.sum(jnp.where(row == col, first, 0.0), axis=0, keepdims=True)
        packed[q, 128:136, :] = jnp.broadcast_to(diag, (8, 128))

    for o in FAR_4 + (0,):
        xo = lax.rem(x + o, NX)
        pair = lax.rem(xo + z, NX)
        copy = remote(packed.at[(1 - core) * 4 + pair], rc.at[xo], c_send.at[o], c_recv.at[o], mate)
        copy.start()
        sends.append(copy)
    for o in FAR_4:
        xo = lax.rem(x + o, NX)
        remote(packed.at[xo], rc.at[xo], c_send.at[o], c_recv.at[o], mate).wait_recv()
        sum4[xo] = packed[core * 4 + lax.rem(xo + z, NX)] + rc[xo]
        copy = remote(sum4.at[xo], rx.at[x], x_send.at[o], x_recv.at[o], x_peers[o])
        copy.start()
        sends.append(copy)
    remote(packed.at[x], rc.at[x], c_send.at[0], c_recv.at[0], mate).wait_recv()
    rx[x] = packed[core * 4 + own] + rc[x]
    for o in FAR_4:
        source = lax.rem(x + NX - o, NX)
        remote(sum4.at[source], rx.at[source], x_send.at[o], x_recv.at[o], x_peers[o]).wait_recv()
    mine = (rx[0] + rx[1]) + (rx[2] + rx[3])

    for i in range(NZ):
        pz[i, 0:16, :] = mine[16 * i : 16 * i + 16]
        pz[i, 16:24, :] = mine[128:136]
    for o in FAR_8:
        zo = lax.rem(z + o, NZ)
        copy = remote(pz.at[zo], rz.at[z], z_send.at[o], z_recv.at[o], z_peers[o])
        copy.start()
        sends.append(copy)
    rz[z] = pz[z]
    for o in FAR_8:
        source = lax.rem(z + NZ - o, NZ)
        remote(pz.at[source], rz.at[source], z_send.at[o], z_recv.at[o], z_peers[o]).wait_recv()
    piece[...] = ((rz[0] + rz[1]) + (rz[2] + rz[3])) + ((rz[4] + rz[5]) + (rz[6] + rz[7]))

    for o in FAR_8:
        copy = remote(piece, ry.at[yy], y_send.at[o], y_recv.at[o], y_peers[o])
        copy.start()
        sends.append(copy)
    ry[yy] = piece[...]
    for o in FAR_8:
        source = lax.rem(yy + NY - o, NY)
        remote(piece, ry.at[source], y_send.at[o], y_recv.at[o], y_peers[o]).wait_recv()
    fin[...] = ((ry[0] + ry[1]) + (ry[2] + ry[3])) + ((ry[4] + ry[5]) + (ry[6] + ry[7]))

    for o in FAR_8:
        copy = remote(fin, gz.at[z], w_send.at[o], w_recv.at[o], z_peers[o])
        copy.start()
        sends.append(copy)
    gz[z] = fin[...]
    for o in FAR_8:
        source = lax.rem(z + NZ - o, NZ)
        remote(fin, gz.at[source], w_send.at[o], w_recv.at[o], z_peers[o]).wait_recv()
    slot = core * 4 + own
    factor(total_rows, gz, held, slot)

    half = (pl.ds(0, 64), pl.ds(64, 64))
    ways = (
        (0, pl.ds(0, 128), x_peers[2], 2),
        (1, half[0], line[2], 2),
        (1, half[1], line[6], 2),
        (0, pl.ds(0, 128), x_peers[1], 3),
        (0, pl.ds(0, 128), x_peers[3], 1),
        (1, pl.ds(0, 128), line[1], 3),
        (1, pl.ds(0, 128), line[7], 1),
    )
    for n, (k, rows, peer, _) in enumerate(ways):
        part = held.at[slot, k, rows]
        copy = remote(part, part, f_send.at[n], f_recv.at[n], peer)
        copy.start()
        sends.append(copy)
    copy = remote(held.at[slot], held.at[slot], m_send.at[7], m_recv.at[7], mate)
    copy.start()
    sends.append(copy)
    order = (3, 4, 5, 6, 0, 1, 2)
    for n in order:
        k, rows, peer, back = ways[n]
        part = held.at[core * 4 + lax.rem(own + back, NX), k, rows]
        remote(part, part, f_send.at[n], f_recv.at[n], peer).wait_recv()
        copy = remote(part, part, m_send.at[n], m_recv.at[n], mate)
        copy.start()
        sends.append(copy)
    theirs = held.at[(1 - core) * 4 + own]
    remote(theirs, theirs, m_send.at[7], m_recv.at[7], mate).wait_recv()
    for n in order:
        k, rows, peer, back = ways[n]
        part = held.at[(1 - core) * 4 + lax.rem(own + back, NX), k, rows]
        remote(part, part, m_send.at[n], m_recv.at[n], mate).wait_recv()
    out[...] = held[...]

    for copy in sends:
        copy.wait_send()
    save.wait()


def over_lanes(a, j):
    return jnp.broadcast_to(a[:, :, j : j + 1], a.shape)


def over_rows(a, i):
    return jnp.broadcast_to(a[:, i : i + 1, :], a.shape)


def factor(total_rows, g, held, slot):
    lanes, subs = iota((1, 8, 128), 2), iota((1, 8, 128), 1)
    row, col = iota((128, 128), 0), iota((128, 128), 1)
    square = jnp.concatenate([g[i, 0:16, :] for i in range(NZ)], axis=0) * (1.0 / total_rows)
    spare = g[0, 16:17, :] * (1.0 / total_rows)
    turned = square.T
    first = jnp.where(row == col, spare, jnp.where(row > col, square, turned))
    second = jnp.where(row > col, turned, square)
    m = [jnp.stack([first[8 * v : 8 * v + 8], second[8 * v : 8 * v + 8]]) for v in range(16)]
    for p in range(16):
        j0 = 8 * p
        top = m[p]
        here = (lanes >= j0) & (lanes < j0 + 8)
        columns = [over_lanes(top, j0 + k) for k in range(8)]
        a = [[over_rows(columns[k], i) for k in range(i + 1)] for i in range(8)]
        for k in range(8):
            r = lax.rsqrt(a[k][k])
            for q in range(k):
                a[k][q] = a[k][q] * r
            a[k][k] = r
            lower = {i: a[i][k] * r for i in range(k + 1, 8)}
            for i in range(k + 1, 8):
                for q in range(k):
                    a[i][q] = a[i][q] - lower[i] * a[k][q]
                a[i][k] = -(lower[i] * r)
                for q in range(k + 1, i + 1):
                    a[i][q] = a[i][q] - lower[i] * lower[q]

        def through(rows):
            done = []
            for i in range(8):
                total = a[i][0] * rows[0]
                for k in range(1, i + 1):
                    total = total + a[i][k] * rows[k]
                done.append(total)
            return done

        def joined(rows):
            whole = rows[7]
            for i in range(7):
                whole = jnp.where(subs == i, rows[i], whole)
            return whole

        base = jnp.where(here, jnp.where(lanes - j0 == subs, 1.0, 0.0), top)
        across = through([over_rows(base, k) for k in range(8)])
        corner = joined(through([over_rows(top, k) for k in range(8)]))
        m[p] = jnp.where(here & (lanes > j0 + subs), corner, joined(across))
        for v in range(p + 1, 16):
            left = through([over_lanes(m[v], j0 + k) for k in range(8)])
            rest = jnp.where(here, 0.0, m[v])
            for i in range(8):
                rest = rest - left[i] * across[i]
            m[v] = rest
    for v in range(16):
        held[slot, :, 8 * v : 8 * v + 8, :] = m[v]


def apply_kernel(pk, zz, upper, basis):
    row, col = iota((128, 128), 0), iota((128, 128), 1)
    for k in range(2):
        both = pk[0, k]
        upper[k] = jnp.where(col > row, both, jnp.where(col == row, 1.0 / both, 0.0))
        inverse = jnp.where(col <= row, both, 0.0)
        high = inverse.astype(BF16)
        low = (inverse - high.astype(F32)).astype(BF16)
        twice = jnp.concatenate([high, high], axis=1)
        found = dot(twice, zz[k]) + dot(low, zz[k, 0:128, :])
        for c in range(3):
            basis[k, c] = found[:, 128 * c : 128 * c + 128].astype(BF16)


def shards(strain, block_starts, bin_numbers):
    vmem = pl.BlockSpec(memory_space=pltpu.VMEM)
    smem = pl.BlockSpec(memory_space=pltpu.SMEM)
    hbm = pl.BlockSpec(memory_space=pl.ANY)
    dma = pltpu.SemaphoreType.DMA
    total_rows = 3.0 * 128 * lax.axis_size("space") * lax.axis_size("tm")
    zz, held = pl.pallas_call(
        functools.partial(first_kernel, total_rows),
        out_shape=(
            jax.ShapeDtypeStruct((16, 256, 384), BF16),
            jax.ShapeDtypeStruct((8, 2, 128, 128), F32),
        ),
        in_specs=[hbm, smem, smem],
        out_specs=(hbm, vmem),
        scratch_shapes=[
            pltpu.VMEM((NT, 3, 264, 128), BF16),
            pltpu.VMEM((8, 384, 128), BF16),
            pltpu.VMEM((256, 512), BF16),
            pltpu.VMEM((8, 256, 384), BF16),
            pltpu.VMEM((32, 64, 128), F32),
            pltpu.VMEM((16, 256, 384), BF16),
            pltpu.VMEM((16, 128, 128), F32),
            pltpu.VMEM((8, 136, 128), F32),
            pltpu.VMEM((4, 136, 128), F32),
            pltpu.VMEM((4, 136, 128), F32),
            pltpu.VMEM((4, 136, 128), F32),
            pltpu.VMEM((NZ, 24, 128), F32),
            pltpu.VMEM((NZ, 24, 128), F32),
            pltpu.VMEM((24, 128), F32),
            pltpu.VMEM((NY, 24, 128), F32),
            pltpu.VMEM((24, 128), F32),
            pltpu.VMEM((NZ, 24, 128), F32),
            pltpu.VMEM((8, 2, 128, 128), F32),
            dma((NT, 3)), dma((NT, 3)), dma,
            dma((4,)), dma((4,)), dma((4,)), dma((4,)),
            dma((8,)), dma((8,)), dma((8,)), dma((8,)), dma((8,)), dma((8,)),
            dma((7,)), dma((7,)), dma((8,)), dma((8,)), dma,
        ],
        compiler_params=pltpu.CompilerParams(
            collective_id=0, has_side_effects=True, vmem_limit_bytes=60 * 1024 * 1024
        ),
    )(strain, block_starts, bin_numbers)
    upper, basis = pl.pallas_call(
        apply_kernel,
        grid=(8,),
        out_shape=(
            jax.ShapeDtypeStruct((16, 128, 128), F32),
            jax.ShapeDtypeStruct((16, 3, 128, 128), BF16),
        ),
        in_specs=[
            pl.BlockSpec((1, 2, 128, 128), lambda i: (i, 0, 0, 0)),
            pl.BlockSpec((2, 256, 384), lambda i: (i, 0, 0)),
        ],
        out_specs=(
            pl.BlockSpec((2, 128, 128), lambda i: (i, 0, 0)),
            pl.BlockSpec((2, 3, 128, 128), lambda i: (i, 0, 0, 0)),
        ),
    )(held, zz)
    return upper, jnp.transpose(basis, (0, 2, 1, 3))


def solution(mesh):
    placed = (P(None, "tm", "space"), P(), P())
    return jax.shard_map(
        shards,
        mesh=mesh,
        in_specs=placed,
        out_specs=(P(), P(None, None, None, ("space", "tm"))),
        check_vma=False,
    )
```

time: 125 us -> 103 us (0.82)
  Pallas kernels: 117 us -> 102 us
  local copies, waits for them, and re-layouts: 6.24 us -> 0 us
    pallas_call x3 -> x1, Pallas kernels: 110 us -> 95.2 us  [shards(): pl.pallas_call(functools.partial(first_kernel, total_rows), out_shape=(ja...]
    unnamed x12 -> x0, local copies, waits for them, and re-layouts: 6.23 us -> none
where the time goes in v2:
time: 103 us
  Pallas kernels  102 us (99%)
    pallas_call x1, Pallas kernels, shards(): pl.pallas_call(functools.partial(first_kernel, total_rows), out_shape=(ja...  95.2 us
    pallas_call x1, Pallas kernels, shards(): pl.pallas_call(apply_kernel, grid=(8,), out_shape=(jax.ShapeDtypeStruct((...  6.97 us

profile of v2, /device:TPU:1, one launch (start us, length us, event | category | flops | bytes accessed | tf_op | source)
XLA Modules:
  0.0 102.9 jit_solution(16830029005146963703)
XLA Ops:
  0.6 95.2 %shard_map.50 = (bf16[16,256,384]{2,1,0:T(8,128)(2,1)}, f32[8,2,128,128]{3,2,1,0:T(8,128)}) custom-call(bf16[3,264,1024]{2,1,0:T(8,128)(2,1)} %strain.1, s32[64]{0:T(128)} %starts.1, s32[16]{0:T(128)} %bins.1), custom_call_target="tpu_custom_call" | custom-call | tf_op jit(solution)/shard_map/pallas_call | solution.py:359
  95.9 7.0 %shard_map.51 = (f32[16,128,128]{2,1,0:T(8,128)}, bf16[16,3,128,128]{3,2,1,0:T(8,128)(2,1)}) custom-call(f32[8,2,128,128]{3,2,1,0:T(8,128)} %get-tuple-element.6.pk, bf16[16,256,384]{2,1,0:T(8,128)(2,1)} %get-tuple-element.7.zz), custom_call_target="tpu_custom_call" | custom-call | tf_op jit(solution)/shard_map/pallas_call | solution.py:395

commit v3 on v2

--- a/solution.py
+++ b/solution.py
@@ -88,7 +88,7 @@
     total_rows,     strain, starts, bins, zout, out,
     came, slab, amat, mmat, spec, zbuf, gram, packed, rc, sum4, rx, pz, rz, piece, ry, fin, gz, held,
     a_send, a_recv, own_sem, c_send, c_recv, x_send, x_recv, z_send, z_recv,
-    y_send, y_recv, w_send, w_recv, f_send, f_recv, m_send, m_recv, out_sem,
+    y_send, y_recv, w_send, w_recv, f_send, f_recv, m_send, m_recv, out_sem, keep_sem,
 ):
     s, t, x, z, ylo, core, yhi = place()
     yy = yhi * 2 + ylo
@@ -134,6 +134,20 @@
     build_windows(starts, bins, amat, mmat)
     slab[...] = jnp.zeros_like(slab)
     stay.wait()
+
+    def square(c, f):
+        rows = spec[pl.ds(2 * f, 2)].reshape(128, 128)
+        high = rows.astype(BF16)
+        low = (rows - high.astype(F32)).astype(BF16)
+        both = jnp.concatenate([high, low], axis=0)
+        zbuf[f, :, 128 * c : 128 * c + 128] = both
+        quad = dot_t(both, both)
+        return (quad[:128, :128] + quad[128:, 128:]) + (quad[:128, 128:] + quad[128:, :128])
+
+    def product(c, f, carry):
+        new = square(c, f)
+        gram[f] = gram[f] + new if c else new
+        return carry
 
     for c in range(3):
         for o in FAR_T:
@@ -152,46 +166,41 @@
             found = dot(mmat[g], slab[g])
             spec[:, 8 * g : 8 * g + 8, :] = found.reshape(32, 8, 128)
 
-        def one(f, carry, c=c):
-            rows = spec[pl.ds(2 * f, 2)].reshape(128, 128)
-            high = rows.astype(BF16)
-            low = (rows - high.astype(F32)).astype(BF16)
-            both = jnp.concatenate([high, low], axis=0)
-            zbuf[f, :, 128 * c : 128 * c + 128] = both
-            quad = dot_t(both, both)
-            new = (quad[:128, :128] + quad[128:, 128:]) + (quad[:128, 128:] + quad[128:, :128])
-            if c == 0:
-                gram[f] = new
-            else:
-                gram[f] = gram[f] + new
-            return carry
-
-        lax.fori_loop(0, 16, one, 0)
-    save = pltpu.make_async_copy(zbuf, zout, out_sem)
-    save.start()
+        if c < 2:
+            lax.fori_loop(0, 16, functools.partial(product, c), 0)
 
     row, col = iota((128, 128), 0), iota((128, 128), 1)
-    for q in range(8):
-        first, second = gram[2 * q], gram[2 * q + 1]
+
+    def finish(q):
+        first = gram[2 * q] + square(2, 2 * q)
+        second = gram[2 * q + 1] + square(2, 2 * q + 1)
         packed[q, 0:128, :] = jnp.where(row > col, first, second)
         diag = jnp.sum(jnp.where(row == col, first, 0.0), axis=0, keepdims=True)
         packed[q, 128:136, :] = jnp.broadcast_to(diag, (8, 128))
 
-    for o in FAR_4 + (0,):
-        xo = lax.rem(x + o, NX)
-        pair = lax.rem(xo + z, NX)
-        copy = remote(packed.at[(1 - core) * 4 + pair], rc.at[xo], c_send.at[o], c_recv.at[o], mate)
-        copy.start()
-        sends.append(copy)
-    for o in FAR_4:
-        xo = lax.rem(x + o, NX)
-        remote(packed.at[xo], rc.at[xo], c_send.at[o], c_recv.at[o], mate).wait_recv()
-        sum4[xo] = packed[core * 4 + lax.rem(xo + z, NX)] + rc[xo]
-        copy = remote(sum4.at[xo], rx.at[x], x_send.at[o], x_recv.at[o], x_peers[o])
-        copy.start()
-        sends.append(copy)
-    remote(packed.at[x], rc.at[x], c_send.at[0], c_recv.at[0], mate).wait_recv()
-    rx[x] = packed[core * 4 + own] + rc[x]
+    there = {o: lax.rem(x + o, NX) for o in FAR_4 + (0,)}
+    theirs = {o: (1 - core) * 4 + lax.rem(there[o] + z, NX) for o in there}
+    ours = {o: core * 4 + lax.rem(there[o] + z, NX) for o in there}
+    for o in there:
+        finish(theirs[o])
+    for o in there:
+        copy = remote(packed.at[theirs[o]], rc.at[there[o]], c_send.at[o], c_recv.at[o], mate)
+        copy.start()
+        sends.append(copy)
+    for o in there:
+        finish(ours[o])
+    for o in there:
+        xo, pair = there[o], ours[o]
+        remote(packed.at[pair], rc.at[xo], c_send.at[o], c_recv.at[o], mate).wait_recv()
+        if o:
+            sum4[xo] = packed[pair] + rc[xo]
+            copy = remote(sum4.at[xo], rx.at[x], x_send.at[o], x_recv.at[o], x_peers[o])
+            copy.start()
+            sends.append(copy)
+        else:
+            rx[x] = packed[pair] + rc[x]
+    save = pltpu.make_async_copy(zbuf, zout, out_sem)
+    save.start()
     for o in FAR_4:
         source = lax.rem(x + NX - o, NX)
         remote(sum4.at[source], rx.at[source], x_send.at[o], x_recv.at[o], x_peers[o]).wait_recv()
@@ -230,45 +239,62 @@
         source = lax.rem(z + NZ - o, NZ)
         remote(fin, gz.at[source], w_send.at[o], w_recv.at[o], z_peers[o]).wait_recv()
     slot = core * 4 + own
-    factor(total_rows, gz, held, slot)
-
-    half = (pl.ds(0, 64), pl.ds(64, 64))
-    ways = (
-        (0, pl.ds(0, 128), x_peers[2], 2),
-        (1, half[0], line[2], 2),
-        (1, half[1], line[6], 2),
-        (0, pl.ds(0, 128), x_peers[1], 3),
-        (0, pl.ds(0, 128), x_peers[3], 1),
-        (1, pl.ds(0, 128), line[1], 3),
-        (1, pl.ds(0, 128), line[7], 1),
-    )
-    for n, (k, rows, peer, _) in enumerate(ways):
-        part = held.at[slot, k, rows]
-        copy = remote(part, part, f_send.at[n], f_recv.at[n], peer)
-        copy.start()
-        sends.append(copy)
-    copy = remote(held.at[slot], held.at[slot], m_send.at[7], m_recv.at[7], mate)
-    copy.start()
-    sends.append(copy)
-    order = (3, 4, 5, 6, 0, 1, 2)
+    ways = []
+    for band, (start, size) in enumerate(((0, 64), (64, 32), (96, 32))):
+        rows = pl.ds(start, size)
+        if band == 0:
+            ways.append((band, 1, pl.ds(0, 32), line[2], 2))
+            ways.append((band, 1, pl.ds(32, 32), line[6], 2))
+        else:
+            ways.append((band, 1, rows, line[2 if band == 1 else 6], 2))
+        ways.append((band, 0, rows, x_peers[2], 2))
+        ways.append((band, 0, rows, x_peers[1], 3))
+        ways.append((band, 0, rows, x_peers[3], 1))
+        ways.append((band, 1, rows, line[1], 3))
+        ways.append((band, 1, rows, line[7], 1))
+    bands = (pl.ds(0, 64), pl.ds(64, 32), pl.ds(96, 32))
+
+    def final(band):
+        for n, (which, k, rows, peer, _) in enumerate(ways):
+            if which == band:
+                part = held.at[slot, k, rows]
+                copy = remote(part, part, f_send.at[n], f_recv.at[n], peer)
+                copy.start()
+                sends.append(copy)
+        part = held.at[slot, :, bands[band]]
+        copy = remote(part, part, m_send.at[20 + band], m_recv.at[20 + band], mate)
+        copy.start()
+        sends.append(copy)
+
+    factor(total_rows, gz, held, slot, final)
+
+    order = [n for band in range(3) for d in (3, 1, 2) for n, w in enumerate(ways) if w[0] == band and w[4] == d]
     for n in order:
-        k, rows, peer, back = ways[n]
+        _, k, rows, peer, back = ways[n]
         part = held.at[core * 4 + lax.rem(own + back, NX), k, rows]
         remote(part, part, f_send.at[n], f_recv.at[n], peer).wait_recv()
         copy = remote(part, part, m_send.at[n], m_recv.at[n], mate)
         copy.start()
         sends.append(copy)
-    theirs = held.at[(1 - core) * 4 + own]
-    remote(theirs, theirs, m_send.at[7], m_recv.at[7], mate).wait_recv()
+    keep = [
+        pltpu.make_async_copy(held.at[pl.ds(q * 4, 4)], out.at[pl.ds(q * 4, 4)], keep_sem.at[n])
+        for n, q in enumerate((core, 1 - core))
+    ]
+    keep[0].start()
+    for band in range(3):
+        part = held.at[(1 - core) * 4 + own, :, bands[band]]
+        remote(part, part, m_send.at[20 + band], m_recv.at[20 + band], mate).wait_recv()
     for n in order:
-        k, rows, peer, back = ways[n]
+        _, k, rows, peer, back = ways[n]
         part = held.at[(1 - core) * 4 + lax.rem(own + back, NX), k, rows]
         remote(part, part, m_send.at[n], m_recv.at[n], mate).wait_recv()
-    out[...] = held[...]
+    keep[1].start()
 
     for copy in sends:
         copy.wait_send()
     save.wait()
+    for copy in keep:
+        copy.wait()
 
 
 def over_lanes(a, j):
@@ -279,7 +305,7 @@
     return jnp.broadcast_to(a[:, i : i + 1, :], a.shape)
 
 
-def factor(total_rows, g, held, slot):
+def factor(total_rows, g, held, slot, final):
     lanes, subs = iota((1, 8, 128), 2), iota((1, 8, 128), 1)
     row, col = iota((128, 128), 0), iota((128, 128), 1)
     square = jnp.concatenate([g[i, 0:16, :] for i in range(NZ)], axis=0) * (1.0 / total_rows)
@@ -325,21 +351,20 @@
         base = jnp.where(here, jnp.where(lanes - j0 == subs, 1.0, 0.0), top)
         across = through([over_rows(base, k) for k in range(8)])
         corner = joined(through([over_rows(top, k) for k in range(8)]))
-        m[p] = jnp.where(here & (lanes > j0 + subs), corner, joined(across))
+        held[slot, :, j0 : j0 + 8, :] = jnp.where(here & (lanes > j0 + subs), corner, joined(across))
+        if p in (7, 11, 15):
+            final((7, 11, 15).index(p))
         for v in range(p + 1, 16):
             left = through([over_lanes(m[v], j0 + k) for k in range(8)])
             rest = jnp.where(here, 0.0, m[v])
             for i in range(8):
                 rest = rest - left[i] * across[i]
             m[v] = rest
-    for v in range(16):
-        held[slot, :, 8 * v : 8 * v + 8, :] = m[v]
-
 
 def apply_kernel(pk, zz, upper, basis):
     row, col = iota((128, 128), 0), iota((128, 128), 1)
-    for k in range(2):
-        both = pk[0, k]
+    for k in range(8):
+        both = pk[k // 2, k % 2]
         upper[k] = jnp.where(col > row, both, jnp.where(col == row, 1.0 / both, 0.0))
         inverse = jnp.where(col <= row, both, 0.0)
         high = inverse.astype(BF16)
@@ -351,7 +376,6 @@
 
 
 def shards(strain, block_starts, bin_numbers):
-    vmem = pl.BlockSpec(memory_space=pltpu.VMEM)
     smem = pl.BlockSpec(memory_space=pltpu.SMEM)
     hbm = pl.BlockSpec(memory_space=pl.ANY)
     dma = pltpu.SemaphoreType.DMA
@@ -363,7 +387,7 @@
             jax.ShapeDtypeStruct((8, 2, 128, 128), F32),
         ),
         in_specs=[hbm, smem, smem],
-        out_specs=(hbm, vmem),
+        out_specs=(hbm, hbm),
         scratch_shapes=[
             pltpu.VMEM((NT, 3, 264, 128), BF16),
             pltpu.VMEM((8, 384, 128), BF16),
@@ -386,7 +410,7 @@
             dma((NT, 3)), dma((NT, 3)), dma,
             dma((4,)), dma((4,)), dma((4,)), dma((4,)),
             dma((8,)), dma((8,)), dma((8,)), dma((8,)), dma((8,)), dma((8,)),
-            dma((7,)), dma((7,)), dma((8,)), dma((8,)), dma,
+            dma((20,)), dma((20,)), dma((23,)), dma((23,)), dma, dma((2,)),
         ],
         compiler_params=pltpu.CompilerParams(
             collective_id=0, has_side_effects=True, vmem_limit_bytes=60 * 1024 * 1024
@@ -394,19 +418,20 @@
     )(strain, block_starts, bin_numbers)
     upper, basis = pl.pallas_call(
         apply_kernel,
-        grid=(8,),
+        grid=(2,),
         out_shape=(
             jax.ShapeDtypeStruct((16, 128, 128), F32),
             jax.ShapeDtypeStruct((16, 3, 128, 128), BF16),
         ),
         in_specs=[
-            pl.BlockSpec((1, 2, 128, 128), lambda i: (i, 0, 0, 0)),
-            pl.BlockSpec((2, 256, 384), lambda i: (i, 0, 0)),
+            pl.BlockSpec((4, 2, 128, 128), lambda i: (i, 0, 0, 0)),
+            pl.BlockSpec((8, 256, 384), lambda i: (i, 0, 0)),
         ],
         out_specs=(
-            pl.BlockSpec((2, 128, 128), lambda i: (i, 0, 0)),
-            pl.BlockSpec((2, 3, 128, 128), lambda i: (i, 0, 0, 0)),
+            pl.BlockSpec((8, 128, 128), lambda i: (i, 0, 0)),
+            pl.BlockSpec((8, 3, 128, 128), lambda i: (i, 0, 0, 0)),
         ),
+        compiler_params=pltpu.CompilerParams(vmem_limit_bytes=32 * 1024 * 1024),
     )(held, zz)
     return upper, jnp.transpose(basis, (0, 2, 1, 3))
 

time: 103 us -> 98 us (0.951)
  Pallas kernels: 102 us -> 94 us
  local copies, waits for them, and re-layouts: 0 us -> 3.11 us
    pallas_call x1, Pallas kernels: 6.97 us -> 2.19 us  [shards(): pl.pallas_call(apply_kernel, grid=(2,), out_shape=(jax.ShapeDtypeStruct((...]
    pallas_call x1, Pallas kernels: 95.2 us -> 91.8 us  [shards(): pl.pallas_call(functools.partial(first_kernel, total_rows), out_shape=(ja...]
    unnamed x0 -> x4, local copies, waits for them, and re-layouts: none -> 3.11 us
where the time goes in v3:
time: 98 us; the launch traced here: 97.8 us
  Pallas kernels  94 us (96%)
  local copies, waits for them, and re-layouts  3.11 us (3%)
    pallas_call x1, Pallas kernels, shards(): pl.pallas_call(functools.partial(first_kernel, total_rows), out_shape=(ja...  91.8 us
    unnamed x4, local copies, waits for them, and re-layouts  3.11 us
    pallas_call x1, Pallas kernels, shards(): pl.pallas_call(apply_kernel, grid=(2,), out_shape=(jax.ShapeDtypeStruct((...  2.19 us

profile of v3, /device:TPU:1, one launch (start us, length us, event | category | flops | bytes accessed | tf_op | source)
XLA Modules:
  0.0 97.8 jit_solution(12962039718665056997)
XLA Ops:
  0.6 91.8 %shard_map.50 = (bf16[16,256,384]{2,1,0:T(8,128)(2,1)}, f32[8,2,128,128]{3,2,1,0:T(8,128)}) custom-call(bf16[3,264,1024]{2,1,0:T(8,128)(2,1)} %strain.1, s32[64]{0:T(128)} %starts.1, s32[16]{0:T(128)} %bins.1), custom_call_target="tpu_custom_call" | custom-call | tf_op jit(solution)/shard_map/pallas_call | solution.py:383
  92.5 0.0 copy-start
  92.5 1.9 %copy-done = bf16[16,256,384]{2,1,0:T(8,128)(2,1)S(1)} copy-done((bf16[16,256,384]{2,1,0:T(8,128)(2,1)S(1)}, bf16[16,256,384]{2,1,0:T(8,128)(2,1)}, u32[]{:S(2)}) %copy-start) | copy-done | bytes 3145752
  94.4 0.0 copy-start.1
  94.4 1.2 %copy-done.1 = f32[8,2,128,128]{3,2,1,0:T(8,128)S(1)} copy-done((f32[8,2,128,128]{3,2,1,0:T(8,128)S(1)}, f32[8,2,128,128]{3,2,1,0:T(8,128)}, u32[]{:S(2)}) %copy-start.1) | copy-done | bytes 1048600
  95.6 2.2 %shard_map.51 = (f32[16,128,128]{2,1,0:T(8,128)}, bf16[16,3,128,128]{3,2,1,0:T(8,128)(2,1)}) custom-call(f32[8,2,128,128]{3,2,1,0:T(8,128)S(1)} %copy-done.1, bf16[16,256,384]{2,1,0:T(8,128)(2,1)S(1)} %copy-done), custom_call_target="tpu_custom_call" | custom-call | tf_op jit(solution)/shard_map/pallas_call | solution.py:419
Async XLA Ops:
  92.5 1.9 %copy-start = (bf16[16,256,384]{2,1,0:T(8,128)(2,1)S(1)}, bf16[16,256,384]{2,1,0:T(8,128)(2,1)}, u32[]{:S(2)}) copy-start(bf16[16,256,384]{2,1,0:T(8,128)(2,1)} %get-tuple-element.7.zz) | copy-start | bytes 9437188
  94.4 1.2 %copy-start.1 = (f32[8,2,128,128]{3,2,1,0:T(8,128)S(1)}, f32[8,2,128,128]{3,2,1,0:T(8,128)}, u32[]{:S(2)}) copy-start(f32[8,2,128,128]{3,2,1,0:T(8,128)} %get-tuple-element.6.pk) | copy-start | bytes 3145732

commit v4 on v3

--- a/solution.py
+++ b/solution.py
@@ -231,13 +231,13 @@
     fin[...] = ((ry[0] + ry[1]) + (ry[2] + ry[3])) + ((ry[4] + ry[5]) + (ry[6] + ry[7]))
 
     for o in FAR_8:
-        copy = remote(fin, gz.at[z], w_send.at[o], w_recv.at[o], z_peers[o])
-        copy.start()
-        sends.append(copy)
-    gz[z] = fin[...]
+        copy = remote(fin.at[pl.ds(0, 16)], gz.at[z], w_send.at[o], w_recv.at[o], z_peers[o])
+        copy.start()
+        sends.append(copy)
+    gz[z] = fin[0:16, :]
     for o in FAR_8:
         source = lax.rem(z + NZ - o, NZ)
-        remote(fin, gz.at[source], w_send.at[o], w_recv.at[o], z_peers[o]).wait_recv()
+        remote(fin.at[pl.ds(0, 16)], gz.at[source], w_send.at[o], w_recv.at[o], z_peers[o]).wait_recv()
     slot = core * 4 + own
     ways = []
     for band, (start, size) in enumerate(((0, 64), (64, 32), (96, 32))):
@@ -266,7 +266,7 @@
         copy.start()
         sends.append(copy)
 
-    factor(total_rows, gz, held, slot, final)
+    factor(total_rows, gz, fin, held, slot, final)
 
     order = [n for band in range(3) for d in (3, 1, 2) for n, w in enumerate(ways) if w[0] == band and w[4] == d]
     for n in order:
@@ -305,11 +305,11 @@
     return jnp.broadcast_to(a[:, i : i + 1, :], a.shape)
 
 
-def factor(total_rows, g, held, slot, final):
+def factor(total_rows, g, fin, held, slot, final):
     lanes, subs = iota((1, 8, 128), 2), iota((1, 8, 128), 1)
     row, col = iota((128, 128), 0), iota((128, 128), 1)
-    square = jnp.concatenate([g[i, 0:16, :] for i in range(NZ)], axis=0) * (1.0 / total_rows)
-    spare = g[0, 16:17, :] * (1.0 / total_rows)
+    square = jnp.concatenate([g[i] for i in range(NZ)], axis=0) * (1.0 / total_rows)
+    spare = fin[16:17, :] * (1.0 / total_rows)
     turned = square.T
     first = jnp.where(row == col, spare, jnp.where(row > col, square, turned))
     second = jnp.where(row > col, turned, square)
@@ -363,19 +363,21 @@
 
 def apply_kernel(pk, zz, upper, basis):
     row, col = iota((128, 128), 0), iota((128, 128), 1)
+    step = pl.program_id(0)
     for k in range(8):
-        both = pk[k // 2, k % 2]
+        both = pk[4 * step + k // 2, k % 2]
         upper[k] = jnp.where(col > row, both, jnp.where(col == row, 1.0 / both, 0.0))
         inverse = jnp.where(col <= row, both, 0.0)
         high = inverse.astype(BF16)
         low = (inverse - high.astype(F32)).astype(BF16)
         twice = jnp.concatenate([high, high], axis=1)
-        found = dot(twice, zz[k]) + dot(low, zz[k, 0:128, :])
+        found = dot(twice, zz[8 * step + k]) + dot(low, zz[8 * step + k, 0:128, :])
         for c in range(3):
             basis[k, c] = found[:, 128 * c : 128 * c + 128].astype(BF16)
 
 
 def shards(strain, block_starts, bin_numbers):
+    vmem = pl.BlockSpec(memory_space=pltpu.VMEM)
     smem = pl.BlockSpec(memory_space=pltpu.SMEM)
     hbm = pl.BlockSpec(memory_space=pl.ANY)
     dma = pltpu.SemaphoreType.DMA
@@ -383,8 +385,8 @@
     zz, held = pl.pallas_call(
         functools.partial(first_kernel, total_rows),
         out_shape=(
-            jax.ShapeDtypeStruct((16, 256, 384), BF16),
-            jax.ShapeDtypeStruct((8, 2, 128, 128), F32),
+            pltpu.VMEM((16, 256, 384), BF16),
+            pltpu.VMEM((8, 2, 128, 128), F32),
         ),
         in_specs=[hbm, smem, smem],
         out_specs=(hbm, hbm),
@@ -405,7 +407,7 @@
             pltpu.VMEM((24, 128), F32),
             pltpu.VMEM((NY, 24, 128), F32),
             pltpu.VMEM((24, 128), F32),
-            pltpu.VMEM((NZ, 24, 128), F32),
+            pltpu.VMEM((NZ, 16, 128), F32),
             pltpu.VMEM((8, 2, 128, 128), F32),
             dma((NT, 3)), dma((NT, 3)), dma,
             dma((4,)), dma((4,)), dma((4,)), dma((4,)),
@@ -413,7 +415,7 @@
             dma((20,)), dma((20,)), dma((23,)), dma((23,)), dma, dma((2,)),
         ],
         compiler_params=pltpu.CompilerParams(
-            collective_id=0, has_side_effects=True, vmem_limit_bytes=60 * 1024 * 1024
+            collective_id=0, has_side_effects=True, vmem_limit_bytes=58 * 1024 * 1024
         ),
     )(strain, block_starts, bin_numbers)
     upper, basis = pl.pallas_call(
@@ -423,15 +425,12 @@
             jax.ShapeDtypeStruct((16, 128, 128), F32),
             jax.ShapeDtypeStruct((16, 3, 128, 128), BF16),
         ),
-        in_specs=[
-            pl.BlockSpec((4, 2, 128, 128), lambda i: (i, 0, 0, 0)),
-            pl.BlockSpec((8, 256, 384), lambda i: (i, 0, 0)),
-        ],
+        in_specs=[vmem, vmem],
         out_specs=(
             pl.BlockSpec((8, 128, 128), lambda i: (i, 0, 0)),
             pl.BlockSpec((8, 3, 128, 128), lambda i: (i, 0, 0, 0)),
         ),
-        compiler_params=pltpu.CompilerParams(vmem_limit_bytes=32 * 1024 * 1024),
+        compiler_params=pltpu.CompilerParams(vmem_limit_bytes=24 * 1024 * 1024),
     )(held, zz)
     return upper, jnp.transpose(basis, (0, 2, 1, 3))
 

time: 98 us -> 93.6 us (0.955)
  local copies, waits for them, and re-layouts: 3.11 us -> 0 us
  Pallas kernels: 94 us -> 92.8 us
    unnamed x4 -> x0, local copies, waits for them, and re-layouts: 3.11 us -> none
    pallas_call x1, Pallas kernels: 91.8 us -> 90.6 us  [shards(): pl.pallas_call(functools.partial(first_kernel, total_rows), out_shape=(pl...]
where the time goes in v4:
time: 93.6 us; the launch traced here: 93.4 us
  Pallas kernels  92.8 us (99%)
    pallas_call x1, Pallas kernels, shards(): pl.pallas_call(functools.partial(first_kernel, total_rows), out_shape=(pl...  90.6 us
    pallas_call x1, Pallas kernels, shards(): pl.pallas_call(apply_kernel, grid=(2,), out_shape=(jax.ShapeDtypeStruct((...  2.18 us

profile of v4, /device:TPU:1, one launch (start us, length us, event | category | flops | bytes accessed | tf_op | source)
XLA Modules:
  0.0 93.4 jit_solution(13122258718833124726)
XLA Ops:
  0.6 90.6 %shard_map.50 = (bf16[16,256,384]{2,1,0:T(8,128)(2,1)S(1)}, f32[8,2,128,128]{3,2,1,0:T(8,128)S(1)}) custom-call(bf16[3,264,1024]{2,1,0:T(8,128)(2,1)} %strain.1, s32[64]{0:T(128)} %starts.1, s32[16]{0:T(128)} %bins.1), custom_call_target="tpu_custom_call" | custom-call | tf_op jit(solution)/shard_map/pallas_call | solution.py:385
  91.2 2.2 %shard_map.51 = (f32[16,128,128]{2,1,0:T(8,128)}, bf16[16,3,128,128]{3,2,1,0:T(8,128)(2,1)}) custom-call(f32[8,2,128,128]{3,2,1,0:T(8,128)S(1)} %get-tuple-element.6.pk, bf16[16,256,384]{2,1,0:T(8,128)(2,1)S(1)} %get-tuple-element.7.zz), custom_call_target="tpu_custom_call" | custom-call | tf_op jit(solution)/shard_map/pallas_call | solution.py:421

commit v5 on v4

--- a/solution.py
+++ b/solution.py
@@ -188,8 +188,9 @@
         copy.start()
         sends.append(copy)
     for o in there:
-        finish(ours[o])
-    for o in there:
+        if o in (2, 3):
+            finish(ours[o])
+            finish(ours[o - 1 if o == 2 else 0])
         xo, pair = there[o], ours[o]
         remote(packed.at[pair], rc.at[xo], c_send.at[o], c_recv.at[o], mate).wait_recv()
         if o:

time: 93.6 us -> 93.8 us (level)
  no operation moved by 1% of the time
where the time goes in v5:
time: 93.8 us; the launch traced here: 93.6 us
  Pallas kernels  93 us (99%)
    pallas_call x1, Pallas kernels, shards(): pl.pallas_call(functools.partial(first_kernel, total_rows), out_shape=(pl...  90.8 us
    pallas_call x1, Pallas kernels, shards(): pl.pallas_call(apply_kernel, grid=(2,), out_shape=(jax.ShapeDtypeStruct((...  2.18 us

profile of v5, /device:TPU:1, one launch (start us, length us, event | category | flops | bytes accessed | tf_op | source)
XLA Modules:
  0.0 93.6 jit_solution(5955412598193673107)
XLA Ops:
  0.6 90.8 %shard_map.50 = (bf16[16,256,384]{2,1,0:T(8,128)(2,1)S(1)}, f32[8,2,128,128]{3,2,1,0:T(8,128)S(1)}) custom-call(bf16[3,264,1024]{2,1,0:T(8,128)(2,1)} %strain.1, s32[64]{0:T(128)} %starts.1, s32[16]{0:T(128)} %bins.1), custom_call_target="tpu_custom_call" | custom-call | tf_op jit(solution)/shard_map/pallas_call | solution.py:386
  91.4 2.2 %shard_map.51 = (f32[16,128,128]{2,1,0:T(8,128)}, bf16[16,3,128,128]{3,2,1,0:T(8,128)(2,1)}) custom-call(f32[8,2,128,128]{3,2,1,0:T(8,128)S(1)} %get-tuple-element.6.pk, bf16[16,256,384]{2,1,0:T(8,128)(2,1)S(1)} %get-tuple-element.7.zz), custom_call_target="tpu_custom_call" | custom-call | tf_op jit(solution)/shard_map/pallas_call | solution.py:422
